TPU v7x, 512 devices: a whole 4x4x16 slice. The times are simulated.
512 devices in a mesh: seq: 64 (over z, x), tp: 8 (over y, core).
Axes of the slice: x: 4, y: 4, z: 16, core: 2. Of those that a mesh axis runs over, the one named last changes fastest.
Arguments:
- tokens: bfloat16 [131072, 1280], P(('seq', 'tp')), may hold values from -48 to 48
- slot_embed: bfloat16 [64, 1280], replicated, may hold values from -1 to 1
- w_in: bfloat16 [64, 1280, 2560], P('seq', None, 'tp'), may hold values from -0.15625 to 0.15625
- w_out: bfloat16 [64, 2560, 1280], P('seq', 'tp'), may hold values from -0.125 to 0.125
- cotangent: bfloat16 [131072, 1280], P(('seq', 'tp')), may hold values from -6 to 6
Outputs:
- layer_output: bfloat16 [131072, 1280], P(('seq', 'tp'))
- grad_tokens: bfloat16 [131072, 1280], P(('seq', 'tp'))
- grad_embed: float32 [64, 1280], P('seq', 'tp')
All inputs are finite; a program needn't handle non-finite values.
Results may differ from a plain program's by a relative error of at most 0.023.
Values may be sent and summed in bfloat16 or wider, within the bound.
A program may use at most 64 MiB of HBM per device.

v0:
```python
import jax
import jax.numpy as jnp
from jax import lax
from jax.sharding import PartitionSpec as P

D = 1280
PATCHES = 256


def normalize_rows(values):
    return values * lax.rsqrt(jnp.mean(values * values, axis=-1, keepdims=True) + 1e-06)


def inner_first(first_operand, second_operand):
    return lax.dot_general(
        first_operand, second_operand, (((0,), (0,)), ((), ())), preferred_element_type=jnp.float32
    )


def send_slots(slot_rows):
    moved_rows = lax.all_to_all(slot_rows, "seq", split_axis=1, concat_axis=0, tiled=True)
    return lax.all_gather(moved_rows, "tp", axis=0, tiled=True)


def return_slots(partial_out):
    summed = lax.psum_scatter(
        partial_out.astype(jnp.bfloat16), "tp", scatter_dimension=0, tiled=True
    ).astype(jnp.float32)
    return lax.all_to_all(
        summed.astype(jnp.bfloat16), "seq", split_axis=0, concat_axis=1, tiled=True
    ).astype(summed.dtype)


def shards(tokens, slot_embed, w_in, w_out, cotangent):
    images = tokens.reshape(-1, PATCHES, D)
    cot_images = cotangent.reshape(-1, PATCHES, D)
    logits = jnp.einsum("ipd,ed->ipe", images, slot_embed, preferred_element_type=jnp.float32)
    column_max = jnp.max(logits, axis=1, keepdims=True)
    column_exp = jnp.exp(logits - column_max)
    dispatch = column_exp / jnp.sum(column_exp, axis=1, keepdims=True)
    dispatch_round = dispatch.astype(jnp.bfloat16)
    slot_inputs = jnp.einsum(
        "ipe,ipd->ied", dispatch_round, images, preferred_element_type=jnp.float32
    )
    normed, norm_pullback = jax.vjp(normalize_rows, slot_inputs)
    normed_round = normed.astype(jnp.bfloat16)
    expert_rows = send_slots(normed_round)
    preact = jnp.einsum("red,edf->ref", expert_rows, w_in, preferred_element_type=jnp.float32)
    hidden = jax.nn.gelu(preact).astype(jnp.bfloat16)
    partial_out = jnp.einsum("ref,efd->red", hidden, w_out, preferred_element_type=jnp.float32)
    slot_outputs = return_slots(partial_out).astype(jnp.bfloat16)
    row_max = jnp.max(logits, axis=2, keepdims=True)
    row_exp = jnp.exp(logits - row_max)
    combine = row_exp / jnp.sum(row_exp, axis=2, keepdims=True)
    combine_round = combine.astype(jnp.bfloat16)
    layer_output = jnp.einsum(
        "ipe,ied->ipd", combine_round, slot_outputs, preferred_element_type=jnp.float32
    ).astype(jnp.bfloat16)
    grad_combine = jnp.einsum(
        "ipd,ied->ipe", cot_images, slot_outputs, preferred_element_type=jnp.float32
    )
    grad_slot_out = jnp.einsum(
        "ipe,ipd->ied", combine_round, cot_images, preferred_element_type=jnp.float32
    ).astype(jnp.bfloat16)
    grad_rows = send_slots(grad_slot_out)
    grad_hidden = jnp.einsum("red,efd->ref", grad_rows, w_out, preferred_element_type=jnp.float32)
    unused_value, gelu_pullback = jax.vjp(jax.nn.gelu, preact)
    grad_preact = gelu_pullback(grad_hidden)[0].astype(jnp.bfloat16)
    grad_partial = jnp.einsum("ref,edf->red", grad_preact, w_in, preferred_element_type=jnp.float32)
    grad_normed = return_slots(grad_partial)
    grad_slot_in = norm_pullback(grad_normed)[0].astype(jnp.bfloat16)
    grad_dispatch = jnp.einsum(
        "ipd,ied->ipe", images, grad_slot_in, preferred_element_type=jnp.float32
    )
    dispatch_inner = jnp.sum(dispatch * grad_dispatch, axis=1, keepdims=True)
    combine_inner = jnp.sum(combine * grad_combine, axis=2, keepdims=True)
    grad_logits = (
        combine * (grad_combine - combine_inner) + dispatch * (grad_dispatch - dispatch_inner)
    ).astype(jnp.bfloat16)
    grad_tokens = (
        jnp.einsum("ipe,ied->ipd", dispatch_round, grad_slot_in, preferred_element_type=jnp.float32)
        + jnp.einsum("ipe,ed->ipd", grad_logits, slot_embed, preferred_element_type=jnp.float32)
    ).astype(jnp.bfloat16)
    flat_logits = grad_logits.reshape(tokens.shape[0], -1)
    owned_count = flat_logits.shape[1] // lax.axis_size("seq")
    embed_total = lax.psum(inner_first(flat_logits, tokens), ("seq", "tp"))
    feature_count = embed_total.shape[1] // lax.axis_size("tp")
    owned_rows = lax.dynamic_slice_in_dim(
        embed_total, lax.axis_index("seq") * owned_count, owned_count, 0
    )
    grad_embed = lax.dynamic_slice_in_dim(
        owned_rows, lax.axis_index("tp") * feature_count, feature_count, 1
    )
    return (layer_output.reshape(tokens.shape), grad_tokens.reshape(tokens.shape), grad_embed)


def solution(mesh):
    return jax.shard_map(
        shards,
        mesh=mesh,
        in_specs=(
            P(("seq", "tp"), None),
            P(),
            P("seq", None, "tp"),
            P("seq", "tp", None),
            P(("seq", "tp"), None),
        ),
        out_specs=(P(("seq", "tp"), None), P(("seq", "tp"), None), P("seq", "tp")),
        check_vma=False,
    )
```

profile of v0, /device:TPU:1, one launch (start us, length us, event | category | flops | bytes accessed | tf_op | source)
XLA Modules:
  0.0 690.5 jit_solution(7136251067515544961)
XLA Ops:
  7.2 1.6 fusion.83
  9.1 1.5 multiply_reduce_fusion
  10.7 0.3 copy.36
  11.0 0.5 broadcast.110
  11.5 1.6 reduce.16
  13.1 34.8 %all_to_all.42 = bf16[64,2,640]{2,1,0:T(2,128)(2,1)S(1)} all-to-all(bf16[64,2,640]{2,1,0:T(2,128)(2,1)S(1)} %reshape.194), channel_id=1, replica_groups=mesh['seq'=64,'tp'=8] {'seq'}, dimensions={0} | all-to-all | bytes 327680 | tf_op jit(solution)/shard_map/all_to_all | solution.py:21
  48.1 0.7 copy.14
  49.1 0.3 copy.35
  49.4 1.6 reduce.18
  51.0 22.5 %all_to_all.43 = bf16[64,2,640]{2,1,0:T(2,128)(2,1)S(1)} all-to-all(bf16[64,2,640]{2,1,0:T(2,128)(2,1)S(1)} %reshape.198), channel_id=1, replica_groups=mesh['seq'=64,'tp'=8] {'seq'}, dimensions={0} | all-to-all | bytes 327680 | tf_op jit(solution)/shard_map/all_to_all | solution.py:21
  73.7 0.7 copy.17
  74.6 1.9 fusion.8
  76.6 32.4 %all-gather.7.cloned.1.call-done = bf16[1,512,1280]{2,1,0:T(8,128)(2,1)} async-done(((bf16[1,64,1280]{2,1,0:T(8,128)(2,1)}), bf16[1,512,1280]{2,1,0:T(8,128)(2,1)}) %all-gather.7.cloned.1.call-update) | async-done | bytes 1310736 | tf_op jit(solution)/shard_map/all_gather | solution.py:22
  109.0 4.1 fusion.1
  113.2 2.0 fusion
  115.2 35.9 %reduce-scatter.5.cloned.1.call-done = bf16[64,1,1280]{2,0,1:T(8,128)(2,1)} async-done(((bf16[512,1,1280]{2,0,1:T(8,128)(2,1)}), bf16[64,1,1280]{2,0,1:T(8,128)(2,1)}) %reduce-scatter.5.cloned.1.call-update) | async-done | bytes 163856 | tf_op jit(solution)/shard_map/reduce_scatter | solution.py:26
  151.2 1.6 reduce.19
  152.8 0.7 reshape.200
  153.5 14.4 %all-to-all-start.3 = ((bf16[64,2,640]{2,1,0:T(2,128)(2,1)}), bf16[64,2,640]{2,1,0:T(2,128)(2,1)S(1)}, u32[]{:S(2)}, u32[]{:S(2)}) async-start(bf16[64,2,640]{2,1,0:T(2,128)(2,1)} %reshape.200), calls=%async_computation.5 | async-start | bytes 327680 | tf_op jit(solution)/shard_map/all_to_all | solution.py:29
  167.8 25.4 %reduce-scatter.3.cloned.1.call-done = bf16[64,1,1280]{2,0,1:T(8,128)(2,1)} async-done(((bf16[512,1,1280]{2,0,1:T(8,128)(2,1)}), bf16[64,1,1280]{2,0,1:T(8,128)(2,1)}) %reduce-scatter.3.cloned.1.call-update) | async-done | bytes 163856 | tf_op jit(solution)/shard_map/reduce_scatter | solution.py:26
  193.2 1.6 reduce.17
  194.9 0.7 reshape.196
  195.6 14.0 %all-to-all-start.1 = ((bf16[64,2,640]{2,1,0:T(2,128)(2,1)}), bf16[64,2,640]{2,1,0:T(2,128)(2,1)S(1)}, u32[]{:S(2)}, u32[]{:S(2)}) async-start(bf16[64,2,640]{2,1,0:T(2,128)(2,1)} %reshape.196), calls=%async_computation.2 | async-start | bytes 327680 | tf_op jit(solution)/shard_map/all_to_all | solution.py:29
  210.0 0.3 convolution_bitcast_fusion
  210.3 0.5 fusion.62
  210.8 14.4 %all-to-all-done.1 = bf16[64,2,640]{2,1,0:T(2,128)(2,1)S(1)} async-done(((bf16[64,2,640]{2,1,0:T(2,128)(2,1)}), bf16[64,2,640]{2,1,0:T(2,128)(2,1)S(1)}, u32[]{:S(2)}, u32[]{:S(2)}) %all-to-all-start.1) | async-done | bytes 163872 | tf_op jit(solution)/shard_map/all_to_all | solution.py:29
  225.4 1.6 multiply_reduce_fusion.2
  227.0 1.0 fusion.84
  228.0 1.3 fusion.2
  229.3 1.2 convolution_convert_fusion.2
  230.5 452.1 %all-reduce.2.cloned.1.call-done = f32[64,1280]{1,0:T(8,128)} async-done(((f32[64,1280]{1,0:T(8,128)}), f32[64,1280]{1,0:T(8,128)}) %all-reduce.2.cloned.1.call-update) | async-done | bytes 327696 | tf_op jit(solution)/shard_map/psum | solution.py:86
  682.6 1.3 dynamic_slice.4
  (35 shorter events, 1.9 us)
Async XLA Ops:
  7.2 101.8 %copy-start = (bf16[1,320,1280]{2,1,0:T(8,128)(2,1)S(1)}, bf16[1,320,1280]{2,1,0:T(8,128)(2,1)}, u32[]{:S(2)}) copy-start(bf16[1,320,1280]{2,1,0:T(8,128)(2,1)} %param.8) | copy-start | bytes 2457604
  7.2 67.5 %all-gather.5.cloned.1.call-start = ((), (), s32[]{:S(2)}) async-start(), calls=%async_computation.9 | async-start | bytes 1474560 | tf_op jit(solution)/shard_map/all_gather | solution.py:22
  10.7 38.2 %copy-start.3 = (bf16[256,1280]{1,0:T(8,128)(2,1)S(1)}, bf16[256,1280]{1,0:T(8,128)(2,1)}, u32[]{:S(2)}) copy-start(bf16[256,1280]{1,0:T(8,128)(2,1)} %param.9) | copy-start | bytes 1966084
  48.8 60.2 %all-gather.7.cloned.1.call-start = ((), (), s32[]{:S(2)}) async-start(), calls=%async_computation.10 | async-start | bytes 1474560 | tf_op jit(solution)/shard_map/all_gather | solution.py:22
  49.1 25.6 %copy-start.4 = (bf16[1,1280,320]{1,2,0:T(8,128)(2,1)S(1)}, bf16[1,1280,320]{1,2,0:T(8,128)(2,1)}, u32[]{:S(2)}) copy-start(bf16[1,1280,320]{1,2,0:T(8,128)(2,1)} %param.7) | copy-start | bytes 2457604
  74.4 76.8 %reduce-scatter.5.cloned.1.call-start = ((), (), s32[]{:S(2)}) async-start(), calls=%async_computation.7 | async-start | bytes 1474560 | tf_op jit(solution)/shard_map/reduce_scatter | solution.py:26
  113.1 80.1 %reduce-scatter.3.cloned.1.call-start = ((), (), s32[]{:S(2)}) async-start(), calls=%async_computation.6 | async-start | bytes 1474560 | tf_op jit(solution)/shard_map/reduce_scatter | solution.py:26
  153.5 42.1 %all-to-all-start.3 = ((bf16[64,2,640]{2,1,0:T(2,128)(2,1)}), bf16[64,2,640]{2,1,0:T(2,128)(2,1)S(1)}, u32[]{:S(2)}, u32[]{:S(2)}) async-start(bf16[64,2,640]{2,1,0:T(2,128)(2,1)} %reshape.200), calls=%async_computation.5 | async-start | bytes 327680 | tf_op jit(solution)/shard_map/all_to_all | solution.py:29
  194.8 15.2 %copy-start.1 = (bf16[256,1280]{1,0:T(8,128)(2,1)S(1)}, bf16[256,1280]{1,0:T(8,128)(2,1)}, u32[]{:S(2)}) copy-start(bf16[256,1280]{1,0:T(8,128)(2,1)} %param.5) | copy-start | bytes 1966084
  195.6 29.7 %all-to-all-start.1 = ((bf16[64,2,640]{2,1,0:T(2,128)(2,1)}), bf16[64,2,640]{2,1,0:T(2,128)(2,1)S(1)}, u32[]{:S(2)}, u32[]{:S(2)}) async-start(bf16[64,2,640]{2,1,0:T(2,128)(2,1)} %reshape.196), calls=%async_computation.2 | async-start | bytes 327680 | tf_op jit(solution)/shard_map/all_to_all | solution.py:29
  209.6 473.1 %all-reduce.2.cloned.1.call-start = ((), (), s32[]{:S(2)}) async-start(), calls=%async_computation.8 | async-start | bytes 655360 | tf_op jit(solution)/shard_map/psum | solution.py:86
  225.3 2.7 copy-start.2
Sparse Core Ops, SparseCore 0:
  48.9 25.6 all-gather.4
  77.3 31.6 all-gather.6
  113.3 37.8 reduce-scatter.4
  153.8 39.3 reduce-scatter.2
  228.1 454.4 all-reduce.1
where the time goes:
time: 691 us
  waiting for transfers between devices  561 us (81%)
  blocking collectives  57.3 us (8%)
  starting transfers between devices  28.6 us (4%)
  matrix products  17.3 us (3%)
  between operations  14 us (2%)
  other arithmetic  7.06 us (1%)
    psum x1, waiting for transfers between devices, shards(): embed_total = lax.psum(inner_first(flat_logits, tokens), ('seq', 'tp'))  452 us
    reduce_scatter x2, waiting for transfers between devices, return_slots(): lax.psum_scatter(partial_out.astype(jnp.bfloat16), 'tp', scatter_dimensio...  61.3 us
    all_to_all x2, blocking collectives, send_slots(): lax.all_to_all(slot_rows, 'seq', split_axis=1, concat_axis=0, tiled=True)  57.3 us
    all_gather x2, waiting for transfers between devices, send_slots(): return lax.all_gather(moved_rows, 'tp', axis=0, tiled=True)  32.6 us
    all_to_all x2, starting transfers between devices, return_slots(): lax.all_to_all(summed.astype(jnp.bfloat16), 'seq', split_axis=0, concat_a...  28.4 us
    all_to_all x2, waiting for transfers between devices, return_slots(): lax.all_to_all(summed.astype(jnp.bfloat16), 'seq', split_axis=0, concat_a...  14.4 us
  transfers between devices with their start and end apart: 7, of which 6 were waited for; matrix products, arithmetic and copies ran while one was open for 2% of the time, Pallas kernels for 0%

commit v1 on v0

--- a/solution.py
+++ b/solution.py
@@ -82,15 +82,9 @@
         + jnp.einsum("ipe,ed->ipd", grad_logits, slot_embed, preferred_element_type=jnp.float32)
     ).astype(jnp.bfloat16)
     flat_logits = grad_logits.reshape(tokens.shape[0], -1)
-    owned_count = flat_logits.shape[1] // lax.axis_size("seq")
-    embed_total = lax.psum(inner_first(flat_logits, tokens), ("seq", "tp"))
-    feature_count = embed_total.shape[1] // lax.axis_size("tp")
-    owned_rows = lax.dynamic_slice_in_dim(
-        embed_total, lax.axis_index("seq") * owned_count, owned_count, 0
-    )
-    grad_embed = lax.dynamic_slice_in_dim(
-        owned_rows, lax.axis_index("tp") * feature_count, feature_count, 1
-    )
+    embed_part = inner_first(flat_logits, tokens)
+    embed_tp = lax.psum_scatter(embed_part, "tp", scatter_dimension=1, tiled=True)
+    grad_embed = lax.psum_scatter(embed_tp, "seq", scatter_dimension=0, tiled=True)
     return (layer_output.reshape(tokens.shape), grad_tokens.reshape(tokens.shape), grad_embed)
 
 

time: 691 us -> 546 us (0.79)
  the two profiles are of different devices: /device:TPU:1 before, /device:TPU:8 now
where the time goes in v1:
time: 546 us; the launch traced here: 545 us
  blocking collectives  340 us (62%)
  waiting for transfers between devices  127 us (23%)
  starting transfers between devices  31.2 us (6%)
  matrix products  17.3 us (3%)
  between operations  14 us (3%)
  local copies, waits for them, and re-layouts  8.89 us (2%)
  other arithmetic  7.06 us (1%)
    unnamed x1, blocking collectives  280 us
    all_to_all x2, blocking collectives, send_slots(): lax.all_to_all(slot_rows, 'seq', split_axis=1, concat_axis=0, tiled=True)  59.8 us
    reduce_scatter x2, waiting for transfers between devices, return_slots(): lax.psum_scatter(partial_out.astype(jnp.bfloat16), 'tp', scatter_dimensio...  58.1 us
    all_to_all x2, starting transfers between devices, return_slots(): lax.all_to_all(summed.astype(jnp.bfloat16), 'seq', split_axis=0, concat_a...  31 us
    all_gather x2, waiting for transfers between devices, send_slots(): return lax.all_gather(moved_rows, 'tp', axis=0, tiled=True)  26.5 us
    unnamed x6, waiting for transfers between devices  24.7 us
    all_to_all x2, waiting for transfers between devices, return_slots(): lax.all_to_all(summed.astype(jnp.bfloat16), 'seq', split_axis=0, concat_a...  17.6 us
  transfers between devices with their start and end apart: 7, of which 5 were waited for; matrix products, arithmetic and copies ran while one was open for 3% of the time, Pallas kernels for 0%

profile of v1, /device:TPU:8, one launch (start us, length us, event | category | flops | bytes accessed | tf_op | source)
XLA Modules:
  0.0 545.1 jit_solution(10315796009451680340)
XLA Ops:
  7.2 1.6 fusion.83
  9.1 1.5 multiply_reduce_fusion
  11.0 0.5 broadcast.110
  11.5 1.6 reduce.16
  13.1 37.3 %all_to_all.42 = bf16[64,2,640]{2,1,0:T(2,128)(2,1)S(1)} all-to-all(bf16[64,2,640]{2,1,0:T(2,128)(2,1)S(1)} %reshape.197), channel_id=1, replica_groups=mesh['seq'=64,'tp'=8] {'seq'}, dimensions={0} | all-to-all | bytes 327680 | tf_op jit(solution)/shard_map/all_to_all | solution.py:21
  50.6 0.7 copy.14
  51.9 1.6 reduce.18
  53.6 22.4 %all_to_all.43 = bf16[64,2,640]{2,1,0:T(2,128)(2,1)S(1)} all-to-all(bf16[64,2,640]{2,1,0:T(2,128)(2,1)S(1)} %reshape.201), channel_id=1, replica_groups=mesh['seq'=64,'tp'=8] {'seq'}, dimensions={0} | all-to-all | bytes 327680 | tf_op jit(solution)/shard_map/all_to_all | solution.py:21
  76.1 0.7 copy.17
  76.9 2.8 fusion.8
  79.7 26.5 %all-gather.7.cloned.1.call-done = bf16[1,512,1280]{2,1,0:T(8,128)(2,1)} async-done(((bf16[1,64,1280]{2,1,0:T(8,128)(2,1)}), bf16[1,512,1280]{2,1,0:T(8,128)(2,1)}) %all-gather.7.cloned.1.call-update) | async-done | bytes 1310736 | tf_op jit(solution)/shard_map/all_gather | solution.py:22
  106.1 4.3 fusion.1
  110.5 1.0 copy-done.5
  111.5 2.0 fusion
  113.5 35.5 %reduce-scatter.8.cloned.1.call-done = bf16[64,1,1280]{2,0,1:T(8,128)(2,1)} async-done(((bf16[512,1,1280]{2,0,1:T(8,128)(2,1)}), bf16[64,1,1280]{2,0,1:T(8,128)(2,1)}) %reduce-scatter.8.cloned.1.call-update) | async-done | bytes 163856 | tf_op jit(solution)/shard_map/reduce_scatter | solution.py:26
  149.0 1.6 reduce.19
  150.6 0.7 reshape.203
  151.3 15.6 %all-to-all-start.3 = ((bf16[64,2,640]{2,1,0:T(2,128)(2,1)}), bf16[64,2,640]{2,1,0:T(2,128)(2,1)S(1)}, u32[]{:S(2)}, u32[]{:S(2)}) async-start(bf16[64,2,640]{2,1,0:T(2,128)(2,1)} %reshape.203), calls=%async_computation.5 | async-start | bytes 327680 | tf_op jit(solution)/shard_map/all_to_all | solution.py:29
  166.9 1.3 dynamic-slice
  168.2 22.6 %reduce-scatter.6.cloned.1.call-done = bf16[64,1,1280]{2,0,1:T(8,128)(2,1)} async-done(((bf16[512,1,1280]{2,0,1:T(8,128)(2,1)}), bf16[64,1,1280]{2,0,1:T(8,128)(2,1)}) %reduce-scatter.6.cloned.1.call-update) | async-done | bytes 163856 | tf_op jit(solution)/shard_map/reduce_scatter | solution.py:26
  190.9 1.6 reduce.17
  192.5 0.7 reshape.199
  193.2 15.4 %all-to-all-start.1 = ((bf16[64,2,640]{2,1,0:T(2,128)(2,1)}), bf16[64,2,640]{2,1,0:T(2,128)(2,1)S(1)}, u32[]{:S(2)}, u32[]{:S(2)}) async-start(bf16[64,2,640]{2,1,0:T(2,128)(2,1)} %reshape.199), calls=%async_computation.2 | async-start | bytes 327680 | tf_op jit(solution)/shard_map/all_to_all | solution.py:29
  209.4 17.6 %all-to-all-done.1 = bf16[64,2,640]{2,1,0:T(2,128)(2,1)S(1)} async-done(((bf16[64,2,640]{2,1,0:T(2,128)(2,1)}), bf16[64,2,640]{2,1,0:T(2,128)(2,1)S(1)}, u32[]{:S(2)}, u32[]{:S(2)}) %all-to-all-start.1) | async-done | bytes 163872 | tf_op jit(solution)/shard_map/all_to_all | solution.py:29
  227.5 1.3 convolution_bitcast_fusion
  228.8 1.2 convolution_convert_fusion.2
  230.0 0.4 fusion.62
  230.4 1.3 fusion.2
  231.7 24.7 %reduce-scatter.10.cloned.1.call-done = f32[160,64]{1,0:T(8,128)} async-done(((f32[1280,64]{1,0:T(8,128)}), f32[160,64]{1,0:T(8,128)}) %reduce-scatter.10.cloned.1.call-update) | async-done | bytes 40976
  256.4 1.0 copy.21
  257.3 280.0 %all-reduce = f32[64,160]{1,0:T(8,128)S(1)} all-reduce(f32[64,160]{1,0:T(8,128)S(1)} %copy.21), channel_id=7, replica_groups=mesh['seq'=64,'tp'=8] {'seq'}, use_global_device_ids=true, to_apply=%region_11.0.clone | all-reduce | flops 10240 | bytes 81920
  537.4 1.2 constant_dynamic-slice_fusion
  (40 shorter events, 2.9 us)
Async XLA Ops:
  7.2 99.0 %copy-start = (bf16[1,320,1280]{2,1,0:T(8,128)(2,1)S(1)}, bf16[1,320,1280]{2,1,0:T(8,128)(2,1)}, u32[]{:S(2)}) copy-start(bf16[1,320,1280]{2,1,0:T(8,128)(2,1)} %param.8) | copy-start | bytes 2457604
  7.2 69.7 %all-gather.5.cloned.1.call-start = ((), (), s32[]{:S(2)}) async-start(), calls=%async_computation.9 | async-start | bytes 1474560 | tf_op jit(solution)/shard_map/all_gather | solution.py:22
  10.7 40.7 %copy-start.3 = (bf16[256,1280]{1,0:T(8,128)(2,1)S(1)}, bf16[256,1280]{1,0:T(8,128)(2,1)}, u32[]{:S(2)}) copy-start(bf16[256,1280]{1,0:T(8,128)(2,1)} %param.9) | copy-start | bytes 1966084
  51.3 54.8 %all-gather.7.cloned.1.call-start = ((), (), s32[]{:S(2)}) async-start(), calls=%async_computation.10 | async-start | bytes 1474560 | tf_op jit(solution)/shard_map/all_gather | solution.py:22
  51.6 25.3 %copy-start.4 = (bf16[1,1280,320]{1,2,0:T(8,128)(2,1)S(1)}, bf16[1,1280,320]{1,2,0:T(8,128)(2,1)}, u32[]{:S(2)}) copy-start(bf16[1,1280,320]{1,2,0:T(8,128)(2,1)} %param.7) | copy-start | bytes 2457604
  76.8 72.2 %reduce-scatter.8.cloned.1.call-start = ((), (), s32[]{:S(2)}) async-start(), calls=%async_computation.8 | async-start | bytes 1474560 | tf_op jit(solution)/shard_map/reduce_scatter | solution.py:26
  110.4 1.1 copy-start.5
  110.4 80.4 %reduce-scatter.6.cloned.1.call-start = ((), (), s32[]{:S(2)}) async-start(), calls=%async_computation.7 | async-start | bytes 1474560 | tf_op jit(solution)/shard_map/reduce_scatter | solution.py:26
  151.3 41.9 %all-to-all-start.3 = ((bf16[64,2,640]{2,1,0:T(2,128)(2,1)}), bf16[64,2,640]{2,1,0:T(2,128)(2,1)S(1)}, u32[]{:S(2)}, u32[]{:S(2)}) async-start(bf16[64,2,640]{2,1,0:T(2,128)(2,1)} %reshape.203), calls=%async_computation.5 | async-start | bytes 327680 | tf_op jit(solution)/shard_map/all_to_all | solution.py:29
  192.5 16.6 %copy-start.1 = (bf16[256,1280]{1,0:T(8,128)(2,1)S(1)}, bf16[256,1280]{1,0:T(8,128)(2,1)}, u32[]{:S(2)}) copy-start(bf16[256,1280]{1,0:T(8,128)(2,1)} %param.5) | copy-start | bytes 1966084
  193.2 33.7 %all-to-all-start.1 = ((bf16[64,2,640]{2,1,0:T(2,128)(2,1)}), bf16[64,2,640]{2,1,0:T(2,128)(2,1)S(1)}, u32[]{:S(2)}, u32[]{:S(2)}) async-start(bf16[64,2,640]{2,1,0:T(2,128)(2,1)} %reshape.199), calls=%async_computation.2 | async-start | bytes 327680 | tf_op jit(solution)/shard_map/all_to_all | solution.py:29
  208.6 47.8 %reduce-scatter.10.cloned.1.call-start = ((), (), s32[]{:S(2)}) async-start(), calls=%async_computation.11 | async-start | bytes 737280
  228.7 1.7 copy-start.2
Sparse Core Ops, SparseCore 0:
  51.5 20.1 all-gather.4
  76.9 29.1 all-gather.6
  110.6 38.3 reduce-scatter.7
  151.7 39.1 reduce-scatter.5
  228.9 27.4 reduce-scatter.9

commit v2 on v1

v2 whole, which is shorter than its diff:
```python
import functools
import math

import jax
import jax.numpy as jnp
from jax import lax
from jax.experimental import pallas as pl
from jax.experimental.pallas import tpu as pltpu
from jax.sharding import PartitionSpec as P

X_CHIPS = 4
CORES = 2
WIDE = 256
MESH = pl.DeviceIdType.MESH
F32 = jnp.float32
BF16 = jnp.bfloat16


def dot(a, b, contract=(1, 0)):
    dims = (((contract[0],), (contract[1],)), ((), ()))
    return lax.dot_general(a, b, dims, preferred_element_type=F32)


def one_hot_swap(outer, inner):
    count = outer * inner
    row = lax.broadcasted_iota(jnp.int32, (count, count), 0)
    column = lax.broadcasted_iota(jnp.int32, (count, count), 1)
    o, i = row // inner, row % inner
    return (column == i * outer + o).astype(F32).astype(BF16)


def gelu_and_slope(u):
    k = math.sqrt(2.0 / math.pi)
    th = jnp.tanh(k * (u + 0.044715 * (u * u * u)))
    half = 0.5 * (1.0 + th)
    slope = half + 0.5 * u * (1.0 - th * th) * (k * (1.0 + 3 * 0.044715 * (u * u)))
    return u * half, slope


def far_first(count):
    return sorted(range(1, count), key=lambda d: -min(d, count - d))


def kernel(names, sizes, *refs):
    nz, nx, ny = sizes
    nt = CORES * ny
    r = dict(zip(names, refs))
    seq, t = lax.axis_index("seq"), lax.axis_index("tp")
    z, x = seq // nx, seq % nx
    y, c = t // CORES, t % CORES
    other = 1 - c
    rows = nz * nx
    width = r["slot_in"].shape[1]
    started = []

    def at_z(p):
        return (p * nx + x, t)

    def at_x(p):
        return (z * nx + p, t)

    def at_y(p):
        return (seq, p * CORES + c)

    def at_y_other(p):
        return (seq, p * CORES + other)

    def at_t(p):
        return (seq, p)

    sibling = (seq, y * CORES + other)

    def copy_to(src, dst, sems, k, device):
        return pltpu.make_async_remote_copy(
            src_ref=src,
            dst_ref=dst,
            send_sem=r[sems + "_s"].at[k],
            recv_sem=r[sems + "_r"].at[k],
            device_id=device,
            device_id_type=MESH,
        )

    def start(*args):
        one = copy_to(*args)
        one.start()
        started.append(one)
        return one

    def exchange(src, dst, me, count, device, sems, order=None):
        copies = []
        for k, d in enumerate(order or range(1, count)):
            peer = lax.rem(me + d, count)
            copies.append(start(src.at[peer], dst.at[me], sems, k, device(peer)))
        dst[pl.ds(me, 1)] = src[pl.ds(me, 1)]
        return copies

    def arrive(copies):
        for one in copies:
            one.wait_recv()

    loads = {}
    for k, name in enumerate(("tokens", "cot", "win", "wout")):
        loads[name] = pltpu.make_async_copy(r[name + "_hbm"], r[name], r["load"].at[k])
        loads[name].start()

    barrier = pltpu.get_barrier_semaphore()
    peers = [at_z(lax.rem(z + d, nz)) for d in range(1, nz)]
    peers += [at_x(lax.rem(x + d, nx)) for d in range(1, nx)]
    peers += [at_t(lax.rem(t + d, nt)) for d in range(1, nt)]
    for peer in peers:
        pl.semaphore_signal(barrier, inc=1, device_id=peer, device_id_type=MESH)

    z_order = far_first(nz)
    loads["tokens"].wait()
    logits = dot(r["embed"][...], r["tokens"][...], (1, 1))
    column_exp = jnp.exp(logits - jnp.max(logits, axis=1, keepdims=True))
    dispatch = column_exp / jnp.sum(column_exp, axis=1, keepdims=True)
    r["dispatch"][...] = dispatch
    slot_in = dot(dispatch.astype(BF16), r["tokens"][...])
    r["slot_in"][...] = slot_in
    scale = lax.rsqrt(jnp.mean(slot_in * slot_in, axis=1, keepdims=True) + 1e-06)
    r["z_out_f"][...] = (slot_in * scale).reshape(nz, nx, width).astype(BF16)
    pl.semaphore_wait(barrier, len(peers))
    z_f = exchange(r["z_out_f"], r["z_in_f"], z, nz, at_z, "z_f", z_order)
    row_exp = jnp.exp(logits - jnp.max(logits, axis=0, keepdims=True))
    combine = row_exp / jnp.sum(row_exp, axis=0, keepdims=True)
    r["combine"][...] = combine
    loads["cot"].wait()
    slot_grad = dot(combine.astype(BF16), r["cot"][...])
    r["z_out_b"][...] = slot_grad.reshape(nz, nx, width).astype(BF16)
    z_b = exchange(r["z_out_b"], r["z_in_b"], z, nz, at_z, "z_b", z_order)

    def spread_x(h, copies):
        arrive(copies)
        held = r["z_in_" + h][...].reshape(rows, width)
        r["x_out_" + h][...] = dot(one_hot_swap(nx, nz), held).astype(BF16).reshape(nx, nz, width)
        return exchange(r["x_out_" + h], r["gather_" + h].at[c, y], x, nx, at_x, "x_" + h)

    def gather_start(h, copies):
        arrive(copies)
        block = r["gather_" + h].at[c, y]
        near = start(block, block, "core_" + h, 0, sibling)
        far = []
        for k, d in enumerate(range(1, ny)):
            far.append(start(block, block, "y_" + h, k, at_y(lax.rem(y + d, ny))))
        return near, far

    def gather_pass(h, far):
        near = []
        for k, d in enumerate(range(1, ny)):
            far[k].wait_recv()
            block = r["gather_" + h].at[c, lax.rem(y + ny - d, ny)]
            near.append(start(block, block, "core_" + h, k + 1, sibling))
        return near

    def expert_inner(h, group):
        held = r["gather_" + h][group].reshape(ny * rows, width)
        if h == "f":
            hidden, slope = gelu_and_slope(dot(held, r["win"][...], (1, 1)))
            r["slope"][group] = slope
            return hidden.astype(BF16)
        return (dot(held, r["wout"][...], (1, 1)) * r["slope"][group]).astype(BF16)

    def expert_outer(h, inner, use):
        weight = r["wout"] if h == "f" else r["win"]
        for low in range(0, width, WIDE):
            cols = pl.ds(low, min(WIDE, width - low))
            use(cols, dot(inner, weight[:, cols]).reshape(ny, rows, -1))

    def expert_near(h):
        def use(cols, part):
            r["half_" + h][:, :, cols] = part.astype(BF16)

        expert_outer(h, expert_inner(h, c), use)
        return start(r["half_" + h], r["half_in_" + h], "half_" + h, 0, sibling)

    def expert_far(h, half):
        inner = expert_inner(h, other)
        half.wait_recv()

        def use(cols, part):
            pair = part + r["half_in_" + h][:, :, cols].astype(F32)
            r["pair_" + h][:, :, cols] = pair.astype(BF16)

        expert_outer(h, inner, use)
        copies = []
        for k, d in enumerate(range(1, ny)):
            peer = lax.rem(y + d, ny)
            copies.append(start(r["pair_" + h].at[peer], r["sum_" + h].at[y], "sum_" + h, k, at_y_other(peer)))
        copies.append(start(r["pair_" + h].at[y], r["sum_" + h].at[y], "sum_" + h, ny - 1, sibling))
        return copies

    def return_x(h, copies):
        arrive(copies)
        total = r["sum_" + h][0].astype(F32)
        for k in range(1, ny):
            total = total + r["sum_" + h][k].astype(F32)
        r["x_back_" + h][...] = total.astype(BF16).reshape(nx, nz, width)
        return exchange(r["x_back_" + h], r["x_home_" + h], x, nx, at_x, "xh_" + h)

    def return_z(h, copies):
        arrive(copies)
        held = r["x_home_" + h][...].reshape(rows, width)
        r["z_back_" + h][...] = dot(one_hot_swap(nz, nx), held).reshape(nz, nx, width).astype(BF16)
        return exchange(r["z_back_" + h], r["z_home_" + h], z, nz, at_z, "zh_" + h, z_order)

    x_f = spread_x("f", z_f)
    near_f, far_f = gather_start("f", x_f)
    x_b = spread_x("b", z_b)
    near_b, far_b = gather_start("b", x_b)
    loads["win"].wait()
    loads["wout"].wait()
    pass_f = gather_pass("f", far_f)
    half_f = expert_near("f")
    arrive([near_f] + pass_f)
    sum_f = expert_far("f", half_f)
    pass_b = gather_pass("b", far_b)
    half_b = expert_near("b")
    arrive([near_b] + pass_b)
    sum_b = expert_far("b", half_b)
    xh_f = return_x("f", sum_f)
    zh_f = return_z("f", xh_f)
    xh_b = return_x("b", sum_b)
    zh_b = return_z("b", xh_b)

    arrive(zh_f)
    combine = r["combine"][...]
    slot_out = r["z_home_f"][...].reshape(rows, width)
    r["out"][...] = dot(combine.T.astype(BF16), slot_out).astype(BF16)
    store_out = pltpu.make_async_copy(r["out"], r["out_hbm"], r["load"].at[4])
    store_out.start()
    grad_combine = dot(slot_out, r["cot"][...], (1, 1))
    combine_inner = jnp.sum(combine * grad_combine, axis=0, keepdims=True)
    grad_logits = combine * (grad_combine - combine_inner)
    slot_in = r["slot_in"][...]
    scale = lax.rsqrt(jnp.mean(slot_in * slot_in, axis=1, keepdims=True) + 1e-06)
    arrive(zh_b)
    grad_normed = r["z_home_b"][...].reshape(rows, width).astype(F32)
    along = jnp.mean(grad_normed * slot_in, axis=1, keepdims=True)
    grad_slot_in = (scale * grad_normed - slot_in * (scale * scale * scale * along)).astype(BF16)
    dispatch = r["dispatch"][...]
    grad_dispatch = dot(grad_slot_in, r["tokens"][...], (1, 1))
    dispatch_inner = jnp.sum(dispatch * grad_dispatch, axis=1, keepdims=True)
    grad_logits = (grad_logits + dispatch * (grad_dispatch - dispatch_inner)).astype(BF16)

    zl = nz // nt
    embed_part = dot(grad_logits, r["tokens"][...])
    r["ge_t_out"][...] = embed_part.reshape(nt, zl * nx, width)
    ge_t = exchange(r["ge_t_out"], r["ge_t_in"], t, nt, at_t, "ge_t")
    both = jnp.concatenate([dispatch.T.astype(BF16), grad_logits.astype(F32).T.astype(BF16)], axis=1)
    right = jnp.concatenate([grad_slot_in, r["embed"][...]], axis=0)
    r["gtok"][...] = dot(both, right).astype(BF16)
    store_gtok = pltpu.make_async_copy(r["gtok"], r["gtok_hbm"], r["load"].at[5])
    store_gtok.start()
    arrive(ge_t)
    owned = jnp.sum(r["ge_t_in"][...], axis=0)
    for lower in range(zl):
        for p in range(nx):
            r["ge_x_out"][p, lower : lower + 1] = owned[lower * nx + p : lower * nx + p + 1]
    ge_x = exchange(r["ge_x_out"], r["ge_x_in"], x, nx, at_x, "ge_x")
    arrive(ge_x)
    owned = jnp.sum(r["ge_x_in"][...], axis=0)
    to_owner = []
    for lower in range(zl):
        r["ge_z_out"][lower] = owned[lower : lower + 1]
    for lower in range(zl):
        owner = t * zl + lower
        one = pltpu.make_async_remote_copy(
            src_ref=r["ge_z_out"].at[lower],
            dst_ref=r["ge_z_in"].at[z],
            send_sem=r["ge_z_s"].at[lower],
            recv_sem=r["ge_z_r"].at[z],
            device_id=at_z(owner),
            device_id_type=MESH,
        )
        to_owner.append((owner, one))

        @pl.when(owner != z)
        def send():
            one.start()

    shares = []
    for k, d in enumerate(range(1, nt)):
        one = pltpu.make_async_remote_copy(
            src_ref=r["ge_row"],
            dst_ref=r["ge_row"],
            send_sem=r["ge_row_s"].at[k],
            recv_sem=r["ge_row_r"].at[0],
            device_id=at_t(lax.rem(t + d, nt)),
            device_id_type=MESH,
        )
        shares.append(one)
    is_owner = z // zl == t

    @pl.when(is_owner)
    def own():
        r["ge_z_in"][pl.ds(z, 1)] = r["ge_z_out"][pl.ds(z - t * zl, 1)]
        for d in range(1, nz):
            source = lax.rem(z + d, nz)
            pltpu.make_async_remote_copy(
                src_ref=r["ge_z_out"].at[0],
                dst_ref=r["ge_z_in"].at[source],
                send_sem=r["ge_z_s"].at[0],
                recv_sem=r["ge_z_r"].at[source],
                device_id=at_z(source),
                device_id_type=MESH,
            ).wait_recv()
        r["ge_row"][...] = jnp.sum(r["ge_z_in"][...], axis=0)
        for one in shares:
            one.start()

    @pl.when(jnp.logical_not(is_owner))
    def take():
        shares[0].wait_recv()

    row = r["ge_row"][...]
    part = width // nt
    mine = row[:, :part]
    for k in range(1, nt):
        mine = jnp.where(t == k, row[:, k * part : (k + 1) * part], mine)
    r["gemb"][...] = mine

    for owner, one in to_owner:

        @pl.when(owner != z)
        def sent():
            one.wait_send()

    @pl.when(is_owner)
    def shared():
        for one in shares:
            one.wait_send()

    store_out.wait()
    store_gtok.wait()
    for one in started:
        one.wait_send()


def solution(mesh):
    nx = X_CHIPS if mesh.shape["seq"] % X_CHIPS == 0 else 1
    nz = mesh.shape["seq"] // nx
    nt = mesh.shape["tp"]
    ny = nt // CORES
    zl = nz // nt
    rows = nz * nx

    def shards(tokens, slot_embed, w_in, w_out, cotangent):
        patches, width = tokens.shape
        inner = w_out.shape[1]
        vmem, dma = pltpu.VMEM, pltpu.SemaphoreType.DMA
        scratch = dict(
            tokens=vmem((patches, width), BF16),
            cot=vmem((patches, width), BF16),
            win=vmem((inner, width), BF16),
            wout=vmem((inner, width), BF16),
            out=vmem((patches, width), BF16),
            gtok=vmem((patches, width), BF16),
            dispatch=vmem((rows, patches), F32),
            combine=vmem((rows, patches), F32),
            slot_in=vmem((rows, width), F32),
            slope=vmem((CORES, ny * rows, inner), F32),
            ge_t_out=vmem((nt, zl * nx, width), F32),
            ge_t_in=vmem((nt, zl * nx, width), F32),
            ge_x_out=vmem((nx, zl, width), F32),
            ge_x_in=vmem((nx, zl, width), F32),
            ge_z_out=vmem((zl, 1, width), F32),
            ge_z_in=vmem((nz, 1, width), F32),
            ge_row=vmem((1, width), F32),
            load=dma((6,)),
            ge_t_s=dma((nt - 1,)),
            ge_t_r=dma((nt - 1,)),
            ge_x_s=dma((nx - 1,)),
            ge_x_r=dma((nx - 1,)),
            ge_z_s=dma((zl,)),
            ge_z_r=dma((nz,)),
            ge_row_s=dma((nt - 1,)),
            ge_row_r=dma((1,)),
        )
        for h in "fb":
            for name in ("z_out", "z_in", "z_back", "z_home"):
                scratch[name + "_" + h] = vmem((nz, nx, width), BF16)
            for name in ("x_out", "x_back", "x_home"):
                scratch[name + "_" + h] = vmem((nx, nz, width), BF16)
            scratch["gather_" + h] = vmem((CORES, ny, nx, nz, width), BF16)
            for name in ("half", "half_in", "pair", "sum"):
                scratch[name + "_" + h] = vmem((ny, rows, width), BF16)
            counts = dict(z=nz - 1, zh=nz - 1, x=nx - 1, xh=nx - 1, y=ny - 1, core=ny, half=1, sum=ny)
            for name, count in counts.items():
                scratch[name + "_" + h + "_s"] = dma((count,))
                scratch[name + "_" + h + "_r"] = dma((count,))
        ins = ["tokens_hbm", "embed", "win_hbm", "wout_hbm", "cot_hbm"]
        outs = ["out_hbm", "gtok_hbm", "gemb"]
        names = ins + outs + list(scratch)
        anywhere = pl.BlockSpec(memory_space=pl.ANY)
        local = pl.BlockSpec(memory_space=pltpu.VMEM)
        return pl.pallas_call(
            functools.partial(kernel, names, (nz, nx, ny)),
            out_shape=(
                jax.ShapeDtypeStruct(tokens.shape, BF16),
                jax.ShapeDtypeStruct(tokens.shape, BF16),
                jax.ShapeDtypeStruct((1, width // nt), F32),
            ),
            in_specs=[anywhere, local, anywhere, anywhere, anywhere],
            out_specs=(anywhere, anywhere, local),
            scratch_shapes=list(scratch.values()),
            compiler_params=pltpu.CompilerParams(
                collective_id=0, has_side_effects=True, vmem_limit_bytes=48 * 1024 * 1024
            ),
        )(tokens, slot_embed, jnp.swapaxes(w_in[0], 0, 1), w_out[0], cotangent)

    return jax.shard_map(
        shards,
        mesh=mesh,
        in_specs=(
            P(("seq", "tp"), None),
            P(),
            P("seq", None, "tp"),
            P("seq", "tp", None),
            P(("seq", "tp"), None),
        ),
        out_specs=(P(("seq", "tp"), None), P(("seq", "tp"), None), P("seq", "tp")),
        check_vma=False,
    )
```

time: 546 us -> 107 us (0.20)
  the two profiles are of different devices: /device:TPU:8 before, /device:TPU:1 now
where the time goes in v2:
time: 107 us
  Pallas kernels  98.5 us (92%)
  local copies, waits for them, and re-layouts  7.61 us (7%)
    pallas_call x1, Pallas kernels, shards(): pl.pallas_call(functools.partial(kernel, names, (nz, nx, ny)), out_shape=...  98.5 us
    unnamed x13, local copies, waits for them, and re-layouts  7.61 us

profile of v2, /device:TPU:1, one launch (start us, length us, event | category | flops | bytes accessed | tf_op | source)
XLA Modules:
  0.0 106.8 jit_solution(17234180141227168695)
XLA Ops:
  0.6 0.0 copy-start
  0.6 1.1 %copy-done = bf16[1,1280,320]{1,2,0:T(8,128)(2,1)S(1)} copy-done((bf16[1,1280,320]{1,2,0:T(8,128)(2,1)S(1)}, bf16[1,1280,320]{1,2,0:T(8,128)(2,1)}, u32[]{:S(2)}) %copy-start) | copy-done | bytes 819224
  1.8 0.0 copy-start.1
  1.8 1.1 %copy-done.1 = bf16[1,320,1280]{2,1,0:T(8,128)(2,1)S(1)} copy-done((bf16[1,320,1280]{2,1,0:T(8,128)(2,1)S(1)}, bf16[1,320,1280]{2,1,0:T(8,128)(2,1)}, u32[]{:S(2)}) %copy-start.1) | copy-done | bytes 819224
  2.9 0.0 copy-start.2
  2.9 1.1 %copy-done.2 = bf16[256,1280]{1,0:T(8,128)(2,1)S(1)} copy-done((bf16[256,1280]{1,0:T(8,128)(2,1)S(1)}, bf16[256,1280]{1,0:T(8,128)(2,1)}, u32[]{:S(2)}) %copy-start.2) | copy-done | bytes 655384
  4.0 0.0 copy-start.3
  4.0 1.1 %copy-done.3 = bf16[256,1280]{1,0:T(8,128)(2,1)S(1)} copy-done((bf16[256,1280]{1,0:T(8,128)(2,1)S(1)}, bf16[256,1280]{1,0:T(8,128)(2,1)}, u32[]{:S(2)}) %copy-start.3) | copy-done | bytes 655384
  5.1 0.0 copy-start.4
  5.1 0.9 copy-done.4
  6.0 98.5 %shard_map.76 = (bf16[256,1280]{1,0:T(8,128)(2,1)S(1)}, bf16[256,1280]{1,0:T(8,128)(2,1)S(1)}, f32[1,160]{1,0:T(1,128)S(1)}) custom-call(bf16[256,1280]{1,0:T(8,128)(2,1)S(1)} %copy-done.2, bf16[64,1280]{1,0:T(8,128)(2,1)S(1)} %copy-done.4, bf16[320,1280]{1,0:T(8,128)(2,1)S(1)} %bitcast.4, bf16[320,1280]{1,0:T(8,128)(2,1)S(1)} %bitcast.5, ...), custom_call_target="tpu_custom_call" | custom-call | tf_op jit(solution)/shard_map/pallas_call | solution.py:397
  104.5 0.8 copy.11
  105.4 0.8 copy.12
  106.2 0.6 copy.13
Async XLA Ops:
  0.6 1.1 %copy-start = (bf16[1,1280,320]{1,2,0:T(8,128)(2,1)S(1)}, bf16[1,1280,320]{1,2,0:T(8,128)(2,1)}, u32[]{:S(2)}) copy-start(bf16[1,1280,320]{1,2,0:T(8,128)(2,1)} %param.7) | copy-start | bytes 2457604
  1.8 1.1 %copy-start.1 = (bf16[1,320,1280]{2,1,0:T(8,128)(2,1)S(1)}, bf16[1,320,1280]{2,1,0:T(8,128)(2,1)}, u32[]{:S(2)}) copy-start(bf16[1,320,1280]{2,1,0:T(8,128)(2,1)} %param.8) | copy-start | bytes 2457604
  2.9 1.1 %copy-start.2 = (bf16[256,1280]{1,0:T(8,128)(2,1)S(1)}, bf16[256,1280]{1,0:T(8,128)(2,1)}, u32[]{:S(2)}) copy-start(bf16[256,1280]{1,0:T(8,128)(2,1)} %refs_0_.1) | copy-start | bytes 1966084
  4.0 1.1 %copy-start.3 = (bf16[256,1280]{1,0:T(8,128)(2,1)S(1)}, bf16[256,1280]{1,0:T(8,128)(2,1)}, u32[]{:S(2)}) copy-start(bf16[256,1280]{1,0:T(8,128)(2,1)} %refs_4_.1) | copy-start | bytes 1966084
  5.1 0.9 copy-start.4

commit v3 on v2

v3 whole, which is shorter than its diff:
```python
import functools
import math

import jax
import jax.numpy as jnp
from jax import lax
from jax.experimental import pallas as pl
from jax.experimental.pallas import tpu as pltpu
from jax.sharding import PartitionSpec as P

X_CHIPS = 4
CORES = 2
WIDE = 256
STEPS = 2
MESH = pl.DeviceIdType.MESH
F32 = jnp.float32
BF16 = jnp.bfloat16


def dot(a, b, contract=(1, 0)):
    dims = (((contract[0],), (contract[1],)), ((), ()))
    return lax.dot_general(a, b, dims, preferred_element_type=F32)


def one_hot_swap(outer, inner):
    count = outer * inner
    row = lax.broadcasted_iota(jnp.int32, (count, count), 0)
    column = lax.broadcasted_iota(jnp.int32, (count, count), 1)
    o, i = row // inner, row % inner
    return (column == i * outer + o).astype(F32).astype(BF16)


def gelu_and_slope(u):
    k = math.sqrt(2.0 / math.pi)
    th = jnp.tanh(k * (u + 0.044715 * (u * u * u)))
    half = 0.5 * (1.0 + th)
    slope = half + 0.5 * u * (1.0 - th * th) * (k * (1.0 + 3 * 0.044715 * (u * u)))
    return u * half, slope


def far_first(count):
    return sorted(range(1, count), key=lambda d: -min(d, count - d))


def kernel(names, sizes, *refs):
    nz, nx, ny = sizes
    nt = CORES * ny
    r = dict(zip(names, refs))
    seq, t = lax.axis_index("seq"), lax.axis_index("tp")
    z, x = seq // nx, seq % nx
    y, c = t // CORES, t % CORES
    rows = nz * nx
    width = r["slot_in"].shape[1]
    started = []

    def at_z(p):
        return (p * nx + x, t)

    def at_xt(p, q):
        return (z * nx + p, q)

    sibling = (seq, y * CORES + 1 - c)

    def copy_to(src, dst, sems, k, device):
        return pltpu.make_async_remote_copy(
            src_ref=src,
            dst_ref=dst,
            send_sem=r[sems + "_s"].at[k],
            recv_sem=r[sems + "_r"].at[k],
            device_id=device,
            device_id_type=MESH,
        )

    def start(*args):
        one = copy_to(*args)
        one.start()
        started.append(one)
        return one

    def exchange(src, dst, sems):
        copies = []
        for k, d in enumerate(far_first(nz)):
            peer = lax.rem(z + d, nz)
            copies.append(start(src.at[peer], dst.at[z], sems, k, at_z(peer)))
        dst[pl.ds(z, 1)] = src[pl.ds(z, 1)]
        return copies

    def arrive(copies):
        for one in copies:
            one.wait_recv()

    inner = r["win_hbm"].shape[0]
    own_inner = pl.ds(pl.multiple_of(c * inner, inner), inner)
    loads = {}
    for k, name in enumerate(("tokens", "cot", "win", "wout")):
        place = r[name].at[own_inner] if name in ("win", "wout") else r[name]
        loads[name] = pltpu.make_async_copy(r[name + "_hbm"], place, r["load"].at[k])
        loads[name].start()

    barrier = pltpu.get_barrier_semaphore()
    peers = [at_z(lax.rem(z + d, nz)) for d in far_first(nz)]
    for d in range(nx):
        peers += [at_xt(lax.rem(x + d, nx), lax.rem(t + e, nt)) for e in range(nt) if d or e]
    for peer in peers:
        pl.semaphore_signal(barrier, inc=1, device_id=peer, device_id_type=MESH)

    loads["tokens"].wait()
    logits = dot(r["embed"][...], r["tokens"][...], (1, 1))
    column_exp = jnp.exp(logits - jnp.max(logits, axis=1, keepdims=True))
    dispatch = column_exp / jnp.sum(column_exp, axis=1, keepdims=True)
    r["dispatch"][...] = dispatch
    slot_in = dot(dispatch.astype(BF16), r["tokens"][...])
    r["slot_in"][...] = slot_in
    scale = lax.rsqrt(jnp.mean(slot_in * slot_in, axis=1, keepdims=True) + 1e-06)
    r["z_out_f"][...] = (slot_in * scale).reshape(nz, nx, width).astype(BF16)
    pl.semaphore_wait(barrier, len(peers))
    z_f = exchange(r["z_out_f"], r["z_in_f"], "z_f")
    row_exp = jnp.exp(logits - jnp.max(logits, axis=0, keepdims=True))
    combine = row_exp / jnp.sum(row_exp, axis=0, keepdims=True)
    r["combine"][...] = combine
    loads["cot"].wait()
    slot_grad = dot(combine.astype(BF16), r["cot"][...])
    r["z_out_b"][...] = slot_grad.reshape(nz, nx, width).astype(BF16)

    plane = [(d, e) for d in range(nx) for e in range(ny)]
    plane.sort(key=lambda step: -min(step[0], nx - step[0]) - min(step[1], ny - step[1]))

    def spread(h, copies):
        arrive(copies)
        held = r["z_in_" + h][...].reshape(rows, width)
        r["x_out_" + h][...] = dot(one_hot_swap(nx, nz), held).astype(BF16).reshape(nx, nz, width)
        mine = r["gather_" + h].at[y, x]
        copies = []
        for k, (d, e) in enumerate(plane[:-1]):
            p, q = lax.rem(x + d, nx), lax.rem(y + e, ny)
            copies.append(start(r["x_out_" + h].at[p], mine, "xy_" + h, k, at_xt(p, q * CORES + c)))
        mine[...] = r["x_out_" + h][x]
        return copies

    def expert(h, copies):
        arrive(copies)
        held = r["gather_" + h][...].reshape(ny * rows, width)
        if h == "f":
            hidden, slope = gelu_and_slope(dot(held, r["win"][...], (1, 1)))
            r["slope"][...] = slope
            weight = r["wout"]
        else:
            hidden = dot(held, r["wout"][...], (1, 1)) * r["slope"][...]
            weight = r["win"]
        hidden = hidden.astype(BF16)
        for low in range(0, width, WIDE):
            cols = pl.ds(low, min(WIDE, width - low))
            part = dot(hidden, weight[:, cols])
            r["part_" + h][:, :, :, cols] = part.astype(BF16).reshape(ny, nx, nz, -1)
        mine = r["sum_" + h].at[y, x]
        copies = []
        for k, (d, e) in enumerate(plane[:-1]):
            p, q = lax.rem(x + d, nx), lax.rem(y + e, ny)
            copies.append(start(r["part_" + h].at[q, p], mine, "sum_" + h, k, at_xt(p, q * CORES + c)))
        mine[...] = r["part_" + h][y, x]
        return copies

    def give_back(h, copies):
        arrive(copies)
        total = r["sum_" + h][0].astype(F32)
        for k in range(1, ny):
            total = total + r["sum_" + h][k].astype(F32)
        held = total.astype(BF16).reshape(rows, width)
        r["z_back_" + h][...] = dot(one_hot_swap(nz, nx), held).reshape(nz, nx, width).astype(BF16)
        return exchange(r["z_back_" + h], r["z_home_" + h], "zh_" + h)

    z_b = exchange(r["z_out_b"], r["z_in_b"], "z_b")
    weights = []
    for k, name in enumerate(("win", "wout")):
        weights.append(start(r[name + "_hbm"], r[name].at[own_inner], "weight", k, sibling))
    xy_f = spread("f", z_f)
    xy_b = spread("b", z_b)
    loads["win"].wait()
    loads["wout"].wait()
    arrive(weights)
    sum_f = expert("f", xy_f)
    sum_b = expert("b", xy_b)
    zh_f = give_back("f", sum_f)
    zh_b = give_back("b", sum_b)

    arrive(zh_f)
    combine = r["combine"][...]
    slot_out = r["z_home_f"][...].reshape(rows, width)
    r["out_left"][...] = combine.T.astype(BF16)
    r["out_right"][...] = slot_out
    grad_combine = dot(slot_out, r["cot"][...], (1, 1))
    combine_inner = jnp.sum(combine * grad_combine, axis=0, keepdims=True)
    grad_logits = combine * (grad_combine - combine_inner)
    slot_in = r["slot_in"][...]
    scale = lax.rsqrt(jnp.mean(slot_in * slot_in, axis=1, keepdims=True) + 1e-06)
    arrive(zh_b)
    grad_normed = r["z_home_b"][...].reshape(rows, width).astype(F32)
    along = jnp.mean(grad_normed * slot_in, axis=1, keepdims=True)
    grad_slot_in = (scale * grad_normed - slot_in * (scale * scale * scale * along)).astype(BF16)
    dispatch = r["dispatch"][...]
    grad_dispatch = dot(grad_slot_in, r["tokens"][...], (1, 1))
    dispatch_inner = jnp.sum(dispatch * grad_dispatch, axis=1, keepdims=True)
    grad_logits = (grad_logits + dispatch * (grad_dispatch - dispatch_inner)).astype(BF16)

    by_x = dot(one_hot_swap(nx, nz), grad_logits).astype(BF16)
    embed_part = dot(by_x, r["tokens"][...]).astype(BF16).reshape(nx, nz, width)
    part = width // nt
    for k in range(nt):
        r["ge_out"][:, k] = embed_part[:, :, k * part : (k + 1) * part]
    ge_xt = []
    mine = r["ge_in"].at[x, t]
    steps = [(d, e) for d in range(nx) for e in range(nt) if d or e]
    for k, (d, e) in enumerate(steps):
        p, q = lax.rem(x + d, nx), lax.rem(t + e, nt)
        ge_xt.append(start(r["ge_out"].at[p, q], mine, "ge_xt", k, at_xt(p, q)))
    mine[...] = r["ge_out"][x, t]
    tok_left = jnp.concatenate([dispatch.astype(BF16).astype(F32), grad_logits.astype(F32)], axis=0)
    r["tok_left"][...] = tok_left.T.astype(BF16)
    r["tok_right"][pl.ds(0, rows)] = grad_slot_in
    r["tok_right"][pl.ds(rows, rows)] = r["embed"][...]
    arrive(ge_xt)
    total = jnp.sum(r["ge_in"][...].astype(F32), axis=(0, 1))
    r["ge_z_out"][...] = total.reshape(nz, 1, part)
    ge_z = exchange(r["ge_z_out"], r["ge_z_in"], "ge_z")
    arrive(ge_z)
    r["gemb"][...] = jnp.sum(r["ge_z_in"][...], axis=0)
    for one in started:
        one.wait_send()


def write_kernel(out_left, out_right, tok_left, tok_right, gemb, out, gtok, gemb_out):
    out[...] = dot(out_left[...], out_right[...]).astype(BF16)
    gtok[...] = dot(tok_left[...], tok_right[...]).astype(BF16)
    gemb_out[...] = gemb[...]


def solution(mesh):
    nx = X_CHIPS if mesh.shape["seq"] % X_CHIPS == 0 else 1
    nz = mesh.shape["seq"] // nx
    nt = mesh.shape["tp"]
    ny = nt // CORES
    rows = nz * nx

    def shards(tokens, slot_embed, w_in, w_out, cotangent):
        patches, width = tokens.shape
        inner = w_out.shape[1]
        vmem, dma = pltpu.VMEM, pltpu.SemaphoreType.DMA
        scratch = dict(
            tokens=vmem((patches, width), BF16),
            cot=vmem((patches, width), BF16),
            win=vmem((CORES * inner, width), BF16),
            wout=vmem((CORES * inner, width), BF16),
            dispatch=vmem((rows, patches), F32),
            combine=vmem((rows, patches), F32),
            slot_in=vmem((rows, width), F32),
            slope=vmem((ny * rows, CORES * inner), F32),
            ge_out=vmem((nx, nt, nz, width // nt), BF16),
            ge_in=vmem((nx, nt, nz, width // nt), BF16),
            ge_z_out=vmem((nz, 1, width // nt), F32),
            ge_z_in=vmem((nz, 1, width // nt), F32),
            load=dma((4,)),
            weight_s=dma((2,)),
            weight_r=dma((2,)),
            ge_xt_s=dma((nx * nt - 1,)),
            ge_xt_r=dma((nx * nt - 1,)),
            ge_z_s=dma((nz - 1,)),
            ge_z_r=dma((nz - 1,)),
        )
        for h in "fb":
            for name in ("z_out", "z_in", "z_back", "z_home"):
                scratch[name + "_" + h] = vmem((nz, nx, width), BF16)
            scratch["x_out_" + h] = vmem((nx, nz, width), BF16)
            for name in ("gather", "part", "sum"):
                scratch[name + "_" + h] = vmem((ny, nx, nz, width), BF16)
            counts = dict(z=nz - 1, zh=nz - 1, xy=nx * ny - 1, sum=nx * ny - 1)
            for name, count in counts.items():
                scratch[name + "_" + h + "_s"] = dma((count,))
                scratch[name + "_" + h + "_r"] = dma((count,))
        ins = ["tokens_hbm", "embed", "win_hbm", "wout_hbm", "cot_hbm"]
        outs = ["out_left", "out_right", "tok_left", "tok_right", "gemb"]
        names = ins + outs + list(scratch)
        anywhere = pl.BlockSpec(memory_space=pl.ANY)
        local = pl.BlockSpec(memory_space=pltpu.VMEM)
        made = pl.pallas_call(
            functools.partial(kernel, names, (nz, nx, ny)),
            out_shape=(
                jax.ShapeDtypeStruct((patches, rows), BF16),
                jax.ShapeDtypeStruct((rows, width), BF16),
                jax.ShapeDtypeStruct((patches, 2 * rows), BF16),
                jax.ShapeDtypeStruct((2 * rows, width), BF16),
                jax.ShapeDtypeStruct((1, width // nt), F32),
            ),
            in_specs=[anywhere, local, anywhere, anywhere, anywhere],
            out_specs=(local,) * 5,
            scratch_shapes=list(scratch.values()),
            compiler_params=pltpu.CompilerParams(
                collective_id=0, has_side_effects=True, vmem_limit_bytes=60 * 1024 * 1024
            ),
        )(tokens, slot_embed, jnp.swapaxes(w_in[0], 0, 1), w_out[0], cotangent)
        step = patches // STEPS
        whole = lambda array: pl.BlockSpec(array.shape, lambda i: (0, 0))
        band = lambda columns: pl.BlockSpec((step, columns), lambda i: (i, 0))
        return pl.pallas_call(
            write_kernel,
            grid=(STEPS,),
            in_specs=[band(rows), whole(made[1]), band(2 * rows), whole(made[3]), whole(made[4])],
            out_specs=(band(width), band(width), whole(made[4])),
            out_shape=(
                jax.ShapeDtypeStruct(tokens.shape, BF16),
                jax.ShapeDtypeStruct(tokens.shape, BF16),
                jax.ShapeDtypeStruct((1, width // nt), F32),
            ),
            compiler_params=pltpu.CompilerParams(vmem_limit_bytes=60 * 1024 * 1024),
        )(*made)

    return jax.shard_map(
        shards,
        mesh=mesh,
        in_specs=(
            P(("seq", "tp"), None),
            P(),
            P("seq", None, "tp"),
            P("seq", "tp", None),
            P(("seq", "tp"), None),
        ),
        out_specs=(P(("seq", "tp"), None), P(("seq", "tp"), None), P("seq", "tp")),
        check_vma=False,
    )
```

time: 107 us -> 91.9 us (0.86)
  local copies, waits for them, and re-layouts: 7.61 us -> 0 us
  Pallas kernels: 98.5 us -> 91.1 us
    pallas_call x1, Pallas kernels: 98.5 us -> 88.6 us  [shards(): pl.pallas_call(functools.partial(kernel, names, (nz, nx, ny)), out_shape=...]
    unnamed x13 -> x0, local copies, waits for them, and re-layouts: 7.61 us -> none
    pallas_call x0 -> x1, Pallas kernels: none -> 2.5 us  [shards(): pl.pallas_call(write_kernel, grid=(STEPS,), in_specs=[band(rows), whole(m...]
where the time goes in v3:
time: 91.9 us; the launch traced here: 91.8 us
  Pallas kernels  91.1 us (99%)
    pallas_call x1, Pallas kernels, shards(): pl.pallas_call(functools.partial(kernel, names, (nz, nx, ny)), out_shape=...  88.6 us
    pallas_call x1, Pallas kernels, shards(): pl.pallas_call(write_kernel, grid=(STEPS,), in_specs=[band(rows), whole(m...  2.5 us

profile of v3, /device:TPU:1, one launch (start us, length us, event | category | flops | bytes accessed | tf_op | source)
XLA Modules:
  0.0 91.8 jit_solution(17378655054328479485)
XLA Ops:
  0.6 88.6 %shard_map.76 = (bf16[256,64]{1,0:T(8,128)(2,1)}, bf16[64,1280]{1,0:T(8,128)(2,1)}, bf16[256,128]{1,0:T(8,128)(2,1)}, bf16[128,1280]{1,0:T(8,128)(2,1)}, f32[1,160]{1,0:T(1,128)}) custom-call(bf16[256,1280]{1,0:T(8,128)(2,1)} %refs_0_.1, bf16[64,1280]{1,0:T(8,128)(2,1)} %refs_1_.1, bf16[320,1280]{1,0:T(8,128)(2,1)} %bitcast.4, bf16[320,1280]{1,0:T(8,128)(2,1)} %bitcast.5, ...), custom_call_target="tpu_custom_call" | custom-call | tf_op jit(solution)/shard_map/pallas_call | solution.py:284
  89.3 2.5 %shard_map.77 = (bf16[256,1280]{1,0:T(8,128)(2,1)}, bf16[256,1280]{1,0:T(8,128)(2,1)}, f32[1,160]{1,0:T(1,128)}) custom-call(bf16[256,64]{1,0:T(8,128)(2,1)} %get-tuple-element.8.out_left, bf16[64,1280]{1,0:T(8,128)(2,1)} %get-tuple-element.9.out_right, bf16[256,128]{1,0:T(8,128)(2,1)} %get-tuple-element.10.tok_left, ...), custom_call_target="tpu_custom_call" | custom-call | tf_op jit(solution)/shard_map/pallas_call | solution.py:303

commit v4 on v3

--- a/solution.py
+++ b/solution.py
@@ -99,8 +99,8 @@
 
     barrier = pltpu.get_barrier_semaphore()
     peers = [at_z(lax.rem(z + d, nz)) for d in far_first(nz)]
-    for d in range(nx):
-        peers += [at_xt(lax.rem(x + d, nx), lax.rem(t + e, nt)) for e in range(nt) if d or e]
+    peers += [at_xt(lax.rem(x + d, nx), lax.rem(y + e, ny) * CORES + c) for d in range(nx) for e in range(ny) if d or e]
+    peers += [sibling]
     for peer in peers:
         pl.semaphore_signal(barrier, inc=1, device_id=peer, device_id_type=MESH)
 
@@ -122,19 +122,36 @@
     slot_grad = dot(combine.astype(BF16), r["cot"][...])
     r["z_out_b"][...] = slot_grad.reshape(nz, nx, width).astype(BF16)
 
+    right, left, across = lax.rem(y + 1, ny), lax.rem(y + ny - 1, ny), lax.rem(y + 2, ny)
+    sides = ((0, 1, right, left), (1, ny - 1, left, right))
+    half = width // 2
     plane = [(d, e) for d in range(nx) for e in range(ny)]
     plane.sort(key=lambda step: -min(step[0], nx - step[0]) - min(step[1], ny - step[1]))
+
+    def row_of_chips(h, src, peer_y, dst, sems, k):
+        copies = []
+        for d in range(nx):
+            p = lax.rem(x + d, nx)
+            if d or peer_y is not y:
+                copies.append(start(src.at[p], dst.at[x], sems + h, k + d, at_xt(p, peer_y * CORES + c)))
+        return copies
 
     def spread(h, copies):
         arrive(copies)
         held = r["z_in_" + h][...].reshape(rows, width)
         r["x_out_" + h][...] = dot(one_hot_swap(nx, nz), held).astype(BF16).reshape(nx, nz, width)
-        mine = r["gather_" + h].at[y, x]
+        mine = r["gather_" + h].at[y]
+        near = [row_of_chips(h, r["x_out_" + h], peer, mine, "xy_", nx * k) for k, _, peer, _ in sides]
+        same = row_of_chips(h, r["x_out_" + h], y, mine, "xy_", 2 * nx)
+        mine[pl.ds(x, 1)] = r["x_out_" + h][pl.ds(x, 1)]
+        return near, same
+
+    def spread_on(h, near):
         copies = []
-        for k, (d, e) in enumerate(plane[:-1]):
-            p, q = lax.rem(x + d, nx), lax.rem(y + e, ny)
-            copies.append(start(r["x_out_" + h].at[p], mine, "xy_" + h, k, at_xt(p, q * CORES + c)))
-        mine[...] = r["x_out_" + h][x]
+        for k, _, peer, source in sides:
+            arrive(near[k])
+            block = r["gather_" + h].at[source, :, :, pl.ds(k * half, half)]
+            copies.append(start(block, block, "xy_" + h, 3 * nx + k, at_xt(x, peer * CORES + c)))
         return copies
 
     def expert(h, copies):
@@ -152,36 +169,53 @@
             cols = pl.ds(low, min(WIDE, width - low))
             part = dot(hidden, weight[:, cols])
             r["part_" + h][:, :, :, cols] = part.astype(BF16).reshape(ny, nx, nz, -1)
-        mine = r["sum_" + h].at[y, x]
         copies = []
-        for k, (d, e) in enumerate(plane[:-1]):
-            p, q = lax.rem(x + d, nx), lax.rem(y + e, ny)
-            copies.append(start(r["part_" + h].at[q, p], mine, "sum_" + h, k, at_xt(p, q * CORES + c)))
-        mine[...] = r["part_" + h][y, x]
-        return copies
+        for k, _, peer, _ in sides:
+            block = r["part_" + h].at[across, :, :, pl.ds(k * half, half)]
+            copies.append(start(block, r["via_" + h].at[k], "sum_" + h, 3 * nx + k, at_xt(x, peer * CORES + c)))
+        mine = r["sum_" + h].at[0]
+        same = row_of_chips(h, r["part_" + h].at[y], y, mine, "sum_", 2 * nx)
+        mine[pl.ds(x, 1)] = r["part_" + h][y, pl.ds(x, 1)]
+        return copies, same
+
+    def sum_on(h, copies):
+        near = []
+        for k, _, peer, _ in sides:
+            arrive([copies[k]])
+            block = r["part_" + h].at[peer, :, :, pl.ds(k * half, half)]
+            block[...] = (block[...].astype(F32) + r["via_" + h][k].astype(F32)).astype(BF16)
+            near += row_of_chips(h, r["part_" + h].at[peer], peer, r["sum_" + h].at[1 + k], "sum_", nx * k)
+        return near
 
     def give_back(h, copies):
         arrive(copies)
         total = r["sum_" + h][0].astype(F32)
-        for k in range(1, ny):
+        for k in range(1, 3):
             total = total + r["sum_" + h][k].astype(F32)
         held = total.astype(BF16).reshape(rows, width)
         r["z_back_" + h][...] = dot(one_hot_swap(nz, nx), held).reshape(nz, nx, width).astype(BF16)
         return exchange(r["z_back_" + h], r["z_home_" + h], "zh_" + h)
 
-    z_b = exchange(r["z_out_b"], r["z_in_b"], "z_b")
     weights = []
     for k, name in enumerate(("win", "wout")):
         weights.append(start(r[name + "_hbm"], r[name].at[own_inner], "weight", k, sibling))
-    xy_f = spread("f", z_f)
-    xy_b = spread("b", z_b)
+    for one in z_f:
+        one.wait_send()
+        started.remove(one)
+    z_b = exchange(r["z_out_b"], r["z_in_b"], "z_b")
+    near_f, same_f = spread("f", z_f)
+    on_f = spread_on("f", near_f)
+    near_b, same_b = spread("b", z_b)
     loads["win"].wait()
     loads["wout"].wait()
     arrive(weights)
-    sum_f = expert("f", xy_f)
-    sum_b = expert("b", xy_b)
-    zh_f = give_back("f", sum_f)
-    zh_b = give_back("b", sum_b)
+    via_f, home_f = expert("f", same_f + on_f)
+    on_b = spread_on("b", near_b)
+    home_f += sum_on("f", via_f)
+    via_b, home_b = expert("b", same_b + on_b)
+    zh_f = give_back("f", home_f)
+    home_b += sum_on("b", via_b)
+    zh_b = give_back("b", home_b)
 
     arrive(zh_f)
     combine = r["combine"][...]
@@ -203,22 +237,25 @@
     grad_logits = (grad_logits + dispatch * (grad_dispatch - dispatch_inner)).astype(BF16)
 
     by_x = dot(one_hot_swap(nx, nz), grad_logits).astype(BF16)
-    embed_part = dot(by_x, r["tokens"][...]).astype(BF16).reshape(nx, nz, width)
+    embed_part = dot(by_x, r["tokens"][...]).astype(BF16)
     part = width // nt
     for k in range(nt):
-        r["ge_out"][:, k] = embed_part[:, :, k * part : (k + 1) * part]
-    ge_xt = []
-    mine = r["ge_in"].at[x, t]
-    steps = [(d, e) for d in range(nx) for e in range(nt) if d or e]
-    for k, (d, e) in enumerate(steps):
-        p, q = lax.rem(x + d, nx), lax.rem(t + e, nt)
-        ge_xt.append(start(r["ge_out"].at[p, q], mine, "ge_xt", k, at_xt(p, q)))
-    mine[...] = r["ge_out"][x, t]
+        r["ge_core"][k % CORES, k // CORES] = embed_part[:, k * part : (k + 1) * part]
+    ge_core = start(r["ge_core"].at[1 - c], r["ge_core_in"], "ge_core", 0, sibling)
     tok_left = jnp.concatenate([dispatch.astype(BF16).astype(F32), grad_logits.astype(F32)], axis=0)
     r["tok_left"][...] = tok_left.T.astype(BF16)
     r["tok_right"][pl.ds(0, rows)] = grad_slot_in
     r["tok_right"][pl.ds(rows, rows)] = r["embed"][...]
-    arrive(ge_xt)
+    arrive([ge_core])
+    pair = r["ge_core"][c].astype(F32) + r["ge_core_in"][...].astype(F32)
+    r["ge_out"][...] = pair.astype(BF16).reshape(ny, nx, nz, part)
+    ge_xy = []
+    mine = r["ge_in"].at[y, x]
+    for k, (d, e) in enumerate(plane[:-1]):
+        p, q = lax.rem(x + d, nx), lax.rem(y + e, ny)
+        ge_xy.append(start(r["ge_out"].at[q, p], mine, "ge_xy", k, at_xt(p, q * CORES + c)))
+    mine[...] = r["ge_out"][y, x]
+    arrive(ge_xy)
     total = jnp.sum(r["ge_in"][...].astype(F32), axis=(0, 1))
     r["ge_z_out"][...] = total.reshape(nz, 1, part)
     ge_z = exchange(r["ge_z_out"], r["ge_z_in"], "ge_z")
@@ -254,15 +291,19 @@
             combine=vmem((rows, patches), F32),
             slot_in=vmem((rows, width), F32),
             slope=vmem((ny * rows, CORES * inner), F32),
-            ge_out=vmem((nx, nt, nz, width // nt), BF16),
-            ge_in=vmem((nx, nt, nz, width // nt), BF16),
+            ge_core=vmem((CORES, ny, rows, width // nt), BF16),
+            ge_core_in=vmem((ny, rows, width // nt), BF16),
+            ge_out=vmem((ny, nx, nz, width // nt), BF16),
+            ge_in=vmem((ny, nx, nz, width // nt), BF16),
             ge_z_out=vmem((nz, 1, width // nt), F32),
             ge_z_in=vmem((nz, 1, width // nt), F32),
             load=dma((4,)),
             weight_s=dma((2,)),
             weight_r=dma((2,)),
-            ge_xt_s=dma((nx * nt - 1,)),
-            ge_xt_r=dma((nx * nt - 1,)),
+            ge_core_s=dma((1,)),
+            ge_core_r=dma((1,)),
+            ge_xy_s=dma((nx * ny - 1,)),
+            ge_xy_r=dma((nx * ny - 1,)),
             ge_z_s=dma((nz - 1,)),
             ge_z_r=dma((nz - 1,)),
         )
@@ -270,9 +311,11 @@
             for name in ("z_out", "z_in", "z_back", "z_home"):
                 scratch[name + "_" + h] = vmem((nz, nx, width), BF16)
             scratch["x_out_" + h] = vmem((nx, nz, width), BF16)
-            for name in ("gather", "part", "sum"):
+            for name in ("gather", "part"):
                 scratch[name + "_" + h] = vmem((ny, nx, nz, width), BF16)
-            counts = dict(z=nz - 1, zh=nz - 1, xy=nx * ny - 1, sum=nx * ny - 1)
+            scratch["sum_" + h] = vmem((3, nx, nz, width), BF16)
+            scratch["via_" + h] = vmem((2, nx, nz, width // 2), BF16)
+            counts = dict(z=nz - 1, zh=nz - 1, xy=3 * nx + 2, sum=3 * nx + 2)
             for name, count in counts.items():
                 scratch[name + "_" + h + "_s"] = dma((count,))
                 scratch[name + "_" + h + "_r"] = dma((count,))

time: 91.9 us -> 87.9 us (0.956)
  Pallas kernels: 91.1 us -> 87.1 us
    pallas_call x1, Pallas kernels: 88.6 us -> 84.6 us  [shards(): pl.pallas_call(functools.partial(kernel, names, (nz, nx, ny)), out_shape=...]
where the time goes in v4:
time: 87.9 us; the launch traced here: 87.7 us
  Pallas kernels  87.1 us (99%)
    pallas_call x1, Pallas kernels, shards(): pl.pallas_call(functools.partial(kernel, names, (nz, nx, ny)), out_shape=...  84.6 us
    pallas_call x1, Pallas kernels, shards(): pl.pallas_call(write_kernel, grid=(STEPS,), in_specs=[band(rows), whole(m...  2.49 us

profile of v4, /device:TPU:1, one launch (start us, length us, event | category | flops | bytes accessed | tf_op | source)
XLA Modules:
  0.0 87.7 jit_solution(8972402637123620878)
XLA Ops:
  0.6 84.6 %shard_map.76 = (bf16[256,64]{1,0:T(8,128)(2,1)}, bf16[64,1280]{1,0:T(8,128)(2,1)}, bf16[256,128]{1,0:T(8,128)(2,1)}, bf16[128,1280]{1,0:T(8,128)(2,1)}, f32[1,160]{1,0:T(1,128)}) custom-call(bf16[256,1280]{1,0:T(8,128)(2,1)} %refs_0_.1, bf16[64,1280]{1,0:T(8,128)(2,1)} %refs_1_.1, bf16[320,1280]{1,0:T(8,128)(2,1)} %bitcast.4, bf16[320,1280]{1,0:T(8,128)(2,1)} %bitcast.5, ...), custom_call_target="tpu_custom_call" | custom-call | tf_op jit(solution)/shard_map/pallas_call | solution.py:327
  85.3 2.5 %shard_map.77 = (bf16[256,1280]{1,0:T(8,128)(2,1)}, bf16[256,1280]{1,0:T(8,128)(2,1)}, f32[1,160]{1,0:T(1,128)}) custom-call(bf16[256,64]{1,0:T(8,128)(2,1)} %get-tuple-element.8.out_left, bf16[64,1280]{1,0:T(8,128)(2,1)} %get-tuple-element.9.out_right, bf16[256,128]{1,0:T(8,128)(2,1)} %get-tuple-element.10.tok_left, ...), custom_call_target="tpu_custom_call" | custom-call | tf_op jit(solution)/shard_map/pallas_call | solution.py:346

commit v5 on v4

--- a/solution.py
+++ b/solution.py
@@ -265,10 +265,26 @@
         one.wait_send()
 
 
-def write_kernel(out_left, out_right, tok_left, tok_right, gemb, out, gtok, gemb_out):
-    out[...] = dot(out_left[...], out_right[...]).astype(BF16)
-    gtok[...] = dot(tok_left[...], tok_right[...]).astype(BF16)
-    gemb_out[...] = gemb[...]
+def write_kernel(*refs):
+    ins, gemb, outs, gemb_out = refs[:4], refs[4], refs[5:7], refs[7]
+    held, made, sems = refs[8:12], refs[12:14], refs[14]
+    loads = [pltpu.make_async_copy(a, b, sems.at[k]) for k, (a, b) in enumerate(zip(ins, held))]
+    for one in loads:
+        one.start()
+    stores = [pltpu.make_async_copy(gemb, gemb_out, sems.at[4])]
+    stores[0].start()
+    step = made[0].shape[0] // STEPS
+    for k in range(2):
+        loads[2 * k].wait()
+        loads[2 * k + 1].wait()
+        for i in range(STEPS):
+            band = pl.ds(i * step, step)
+            made[k][band] = dot(held[2 * k][band], held[2 * k + 1][...]).astype(BF16)
+            one = pltpu.make_async_copy(made[k].at[band], outs[k].at[band], sems.at[5 + k * STEPS + i])
+            one.start()
+            stores.append(one)
+    for one in stores:
+        one.wait()
 
 
 def solution(mesh):
@@ -340,14 +356,13 @@
                 collective_id=0, has_side_effects=True, vmem_limit_bytes=60 * 1024 * 1024
             ),
         )(tokens, slot_embed, jnp.swapaxes(w_in[0], 0, 1), w_out[0], cotangent)
-        step = patches // STEPS
-        whole = lambda array: pl.BlockSpec(array.shape, lambda i: (0, 0))
-        band = lambda columns: pl.BlockSpec((step, columns), lambda i: (i, 0))
         return pl.pallas_call(
             write_kernel,
-            grid=(STEPS,),
-            in_specs=[band(rows), whole(made[1]), band(2 * rows), whole(made[3]), whole(made[4])],
-            out_specs=(band(width), band(width), whole(made[4])),
+            in_specs=[anywhere] * 5,
+            out_specs=(anywhere,) * 3,
+            scratch_shapes=[vmem(array.shape, BF16) for array in made[:4]]
+            + [vmem(tokens.shape, BF16)] * 2
+            + [dma((5 + 2 * STEPS,))],
             out_shape=(
                 jax.ShapeDtypeStruct(tokens.shape, BF16),
                 jax.ShapeDtypeStruct(tokens.shape, BF16),

time: 87.9 us -> 87.9 us (level)
  no operation moved by 1% of the time
where the time goes in v5:
time: 87.9 us; the launch traced here: 87.7 us
  Pallas kernels  87 us (99%)
    pallas_call x1, Pallas kernels, shards(): pl.pallas_call(functools.partial(kernel, names, (nz, nx, ny)), out_shape=...  84.6 us
    pallas_call x1, Pallas kernels, shards(): pl.pallas_call(write_kernel, in_specs=[anywhere] * 5, out_specs=(anywhere...  2.42 us

profile of v5, /device:TPU:1, one launch (start us, length us, event | category | flops | bytes accessed | tf_op | source)
XLA Modules:
  0.0 87.7 jit_solution(16905219458077730586)
XLA Ops:
  0.6 84.6 %shard_map.76 = (bf16[256,64]{1,0:T(8,128)(2,1)}, bf16[64,1280]{1,0:T(8,128)(2,1)}, bf16[256,128]{1,0:T(8,128)(2,1)}, bf16[128,1280]{1,0:T(8,128)(2,1)}, f32[1,160]{1,0:T(1,128)}) custom-call(bf16[256,1280]{1,0:T(8,128)(2,1)} %refs_0_.1, bf16[64,1280]{1,0:T(8,128)(2,1)} %refs_1_.1, bf16[320,1280]{1,0:T(8,128)(2,1)} %bitcast.4, bf16[320,1280]{1,0:T(8,128)(2,1)} %bitcast.5, ...), custom_call_target="tpu_custom_call" | custom-call | tf_op jit(solution)/shard_map/pallas_call | solution.py:343
  85.3 2.4 %shard_map.77 = (bf16[256,1280]{1,0:T(8,128)(2,1)}, bf16[256,1280]{1,0:T(8,128)(2,1)}, f32[1,160]{1,0:T(1,128)}) custom-call(bf16[256,64]{1,0:T(8,128)(2,1)} %get-tuple-element.8.refs_0_, bf16[64,1280]{1,0:T(8,128)(2,1)} %get-tuple-element.9.refs_1_, bf16[256,128]{1,0:T(8,128)(2,1)} %get-tuple-element.10.refs_2_, ...), custom_call_target="tpu_custom_call" | custom-call | tf_op jit(solution)/shard_map/pallas_call | solution.py:359

commit v6 on v5

--- a/solution.py
+++ b/solution.py
@@ -91,18 +91,18 @@
 
     inner = r["win_hbm"].shape[0]
     own_inner = pl.ds(pl.multiple_of(c * inner, inner), inner)
-    loads = {}
-    for k, name in enumerate(("tokens", "cot", "win", "wout")):
-        place = r[name].at[own_inner] if name in ("win", "wout") else r[name]
-        loads[name] = pltpu.make_async_copy(r[name + "_hbm"], place, r["load"].at[k])
-        loads[name].start()
-
     barrier = pltpu.get_barrier_semaphore()
     peers = [at_z(lax.rem(z + d, nz)) for d in far_first(nz)]
     peers += [at_xt(lax.rem(x + d, nx), lax.rem(y + e, ny) * CORES + c) for d in range(nx) for e in range(ny) if d or e]
     peers += [sibling]
     for peer in peers:
         pl.semaphore_signal(barrier, inc=1, device_id=peer, device_id_type=MESH)
+
+    loads = {}
+    for k, name in enumerate(("tokens", "cot", "win", "wout")):
+        place = r[name].at[own_inner] if name in ("win", "wout") else r[name]
+        loads[name] = pltpu.make_async_copy(r[name + "_hbm"], place, r["load"].at[k])
+        loads[name].start()
 
     loads["tokens"].wait()
     logits = dot(r["embed"][...], r["tokens"][...], (1, 1))
@@ -196,13 +196,13 @@
         r["z_back_" + h][...] = dot(one_hot_swap(nz, nx), held).reshape(nz, nx, width).astype(BF16)
         return exchange(r["z_back_" + h], r["z_home_" + h], "zh_" + h)
 
-    weights = []
-    for k, name in enumerate(("win", "wout")):
-        weights.append(start(r[name + "_hbm"], r[name].at[own_inner], "weight", k, sibling))
     for one in z_f:
         one.wait_send()
         started.remove(one)
     z_b = exchange(r["z_out_b"], r["z_in_b"], "z_b")
+    weights = []
+    for k, name in enumerate(("win", "wout")):
+        weights.append(start(r[name + "_hbm"], r[name].at[own_inner], "weight", k, sibling))
     near_f, same_f = spread("f", z_f)
     on_f = spread_on("f", near_f)
     near_b, same_b = spread("b", z_b)

time: 87.9 us -> 88 us (level)
  no operation moved by 1% of the time
where the time goes in v6:
time: 88 us; the launch traced here: 87.8 us
  Pallas kernels  87.2 us (99%)
    pallas_call x1, Pallas kernels, shards(): pl.pallas_call(functools.partial(kernel, names, (nz, nx, ny)), out_shape=...  84.8 us
    pallas_call x1, Pallas kernels, shards(): pl.pallas_call(write_kernel, in_specs=[anywhere] * 5, out_specs=(anywhere...  2.43 us

profile of v6, /device:TPU:1, one launch (start us, length us, event | category | flops | bytes accessed | tf_op | source)
XLA Modules:
  0.0 87.8 jit_solution(15541367330648618668)
XLA Ops:
  0.6 84.8 %shard_map.76 = (bf16[256,64]{1,0:T(8,128)(2,1)}, bf16[64,1280]{1,0:T(8,128)(2,1)}, bf16[256,128]{1,0:T(8,128)(2,1)}, bf16[128,1280]{1,0:T(8,128)(2,1)}, f32[1,160]{1,0:T(1,128)}) custom-call(bf16[256,1280]{1,0:T(8,128)(2,1)} %refs_0_.1, bf16[64,1280]{1,0:T(8,128)(2,1)} %refs_1_.1, bf16[320,1280]{1,0:T(8,128)(2,1)} %bitcast.4, bf16[320,1280]{1,0:T(8,128)(2,1)} %bitcast.5, ...), custom_call_target="tpu_custom_call" | custom-call | tf_op jit(solution)/shard_map/pallas_call | solution.py:343
  85.4 2.4 %shard_map.77 = (bf16[256,1280]{1,0:T(8,128)(2,1)}, bf16[256,1280]{1,0:T(8,128)(2,1)}, f32[1,160]{1,0:T(1,128)}) custom-call(bf16[256,64]{1,0:T(8,128)(2,1)} %get-tuple-element.8.refs_0_, bf16[64,1280]{1,0:T(8,128)(2,1)} %get-tuple-element.9.refs_1_, bf16[256,128]{1,0:T(8,128)(2,1)} %get-tuple-element.10.refs_2_, ...), custom_call_target="tpu_custom_call" | custom-call | tf_op jit(solution)/shard_map/pallas_call | solution.py:359
